TPU v7x, 128 devices: a whole 4x4x4 slice. The times are simulated.
128 devices in a mesh: walker: 16 (over x, y_hi, core), prow: 2 (over y_lo), pcol: 4 (over z).
Axes of the slice: x: 4, y: 4 (y_hi: 2, y_lo: 2; y = y_hi * 2 + y_lo), z: 4, core: 2. Of those that a mesh axis runs over, the one named last changes fastest.
Arguments:
- o_rows: bfloat16 [32768, 2048], P('walker', ('prow', 'pcol')), may hold values from -21 to 21
- o_cols: bfloat16 [32768, 4096], P('walker', ('pcol', 'prow')), may hold values from -48 to 48
- grad_energy: bfloat16 [32768, 4096], P('walker', ('pcol', 'prow')), may hold values from -8 to 8
- energy: float32 [32768], P('walker'), may hold values from -5 to 1
Outputs:
- hamil: float32 [2048, 4096], P(('prow', 'walker'), 'pcol')
- correlation: float32 [2048, 4096], P(('prow', 'walker'), 'pcol')
All inputs are finite; a program needn't handle non-finite values.
Results may differ from a plain program's by a relative error of at most 0.008.
Values may be sent and summed in bfloat16 or wider, within the bound.
A program may use at most 128 MiB of HBM per device.

v0:
```python
import jax
import jax.numpy as jnp
from jax import lax
from jax.sharding import PartitionSpec as P


def column_sums(values):
    return jnp.sum(values.astype(jnp.float32), axis=0)


def tile_product(row_tile, right_tile):
    return lax.dot_general(
        row_tile, right_tile, (((0,), (0,)), ((), ())), preferred_element_type=jnp.float32
    )


def per_device(o_rows, o_cols, grad_energy, energy):
    count = energy.shape[0] * lax.axis_size("walker")
    row_total, col_total = lax.psum((column_sums(o_rows), column_sums(o_cols)), "walker")
    row_shard = (o_rows - row_total / count).astype(jnp.bfloat16)
    col_shard = (o_cols - col_total / count).astype(jnp.bfloat16)
    row_tile = lax.all_gather(row_shard, "pcol", axis=1, tiled=True)
    col_tile, grad_tile = (
        lax.all_gather(col_shard, "prow", axis=1, tiled=True),
        lax.all_gather(grad_energy, "prow", axis=1, tiled=True),
    )
    weighted = (energy[:, None] * col_tile + grad_tile).astype(jnp.bfloat16)
    paired = jnp.concatenate((col_tile, weighted), axis=1)
    summed = lax.psum_scatter(
        tile_product(row_tile, paired), "walker", scatter_dimension=0, tiled=True
    )
    width = col_tile.shape[1]
    correlation = summed[:, :width]
    hamil = summed[:, width:]
    return (hamil / count, correlation / count)


def solution(mesh):
    in_specs = (
        P("walker", ("prow", "pcol")),
        P("walker", ("pcol", "prow")),
        P("walker", ("pcol", "prow")),
        P("walker"),
    )
    out_specs = (P(("prow", "walker"), "pcol"), P(("prow", "walker"), "pcol"))
    return jax.shard_map(
        per_device, mesh=mesh, in_specs=in_specs, out_specs=out_specs, check_vma=False
    )
```

profile of v0, /device:TPU:20, one launch (start us, length us, event | category | flops | bytes accessed | tf_op | source)
XLA Modules:
  0.0 311.4 jit_solution(17419922395982080322)
XLA Ops:
  7.2 0.0 copy-start
  7.2 0.0 all-gather.8.cloned.1.call-start
  7.2 0.7 all-gather.8.cloned.1.call-update
  7.9 0.0 all-gather.6.cloned.1.call-start
  8.0 1.5 convert_reduce_fusion.1
  9.5 0.0 copy-done
  9.5 0.0 copy-start.1
  9.5 0.3 convert_reduce_fusion
  9.8 26.9 %all-reduce = (f32[256]{0:T(256)S(1)}, f32[512]{0:T(512)S(1)}) all-reduce(f32[256]{0:T(256)S(1)} %convert_reduce_fusion.1, f32[512]{0:T(512)S(1)} %convert_reduce_fusion), channel_id=1, replica_groups=mesh['walker'=16,'prow'=2,'pcol'=4] {'walker'}, use_global_device_ids=true, to_apply=%region_1.0 | all-reduce | flops 768 | bytes 6144 | tf_op jit(solution)/shard_map/psum | solution.py:19
  36.7 0.0 copy-start.2
  36.7 1.8 fusion.4
  38.5 0.0 all-gather.6.cloned.1.call-update
  38.5 0.0 all-gather.4.cloned.1.call-start
  38.6 0.0 copy-done.1
  38.6 1.2 fusion.5
  39.8 0.0 all-gather.4.cloned.1.call-update
  39.8 0.0 reduce-scatter.2.cloned.1.call-start
  39.9 31.3 %all-gather.8.cloned.1.call-done = bf16[2048,1024]{1,0:T(8,128)(2,1)} async-done(((bf16[2048,512]{1,0:T(8,128)(2,1)}), bf16[2048,1024]{1,0:T(8,128)(2,1)}) %all-gather.8.cloned.1.call-update) | async-done | bytes 4194320 | tf_op jit(solution)/shard_map/all_gather | solution.py:25
  71.1 62.0 %all-gather.6.cloned.1.call-done = bf16[2048,1024]{1,0:T(8,128)(2,1)} async-done(((bf16[2048,512]{1,0:T(8,128)(2,1)}), bf16[2048,1024]{1,0:T(8,128)(2,1)}) %all-gather.6.cloned.1.call-update) | async-done | bytes 4194320 | tf_op jit(solution)/shard_map/all_gather | solution.py:24
  133.1 0.0 copy-done.2
  133.1 5.4 %add_convert_fusion = bf16[2048,1024]{1,0:T(8,128)(2,1)} fusion(bf16[2048,1024]{1,0:T(8,128)(2,1)} %all-gather.8.cloned.1.call-done, bf16[2048,1024]{1,0:T(8,128)(2,1)} %all-gather.6.cloned.1.call-done, f32[2048]{0:T(1024)S(1)} %copy-done.2), kind=kLoop, calls=%fused_computation.4 | loop fusion | flops 10485760 | bytes 12591104 | tf_op jit(solution)/shard_map/convert_element_type | solution.py:27
  138.6 49.7 %all-gather.4.cloned.1.call-done = bf16[2048,1024]{1,0:T(8,128)(2,1)} async-done(((bf16[2048,256]{1,0:T(8,128)(2,1)}), bf16[2048,1024]{1,0:T(8,128)(2,1)}) %all-gather.4.cloned.1.call-update) | async-done | bytes 4194320 | tf_op jit(solution)/shard_map/all_gather | solution.py:22
  188.3 15.2 %fusion = f32[1024,2048]{1,0:T(8,128)} fusion(bf16[2048,1024]{1,0:T(8,128)(2,1)} %all-gather.4.cloned.1.call-done, bf16[2048,1024]{1,0:T(8,128)(2,1)} %add_convert_fusion, bf16[2048,1024]{1,0:T(8,128)(2,1)} %all-gather.6.cloned.1.call-done), kind=kOutput, calls=%fused_computation | convolution fusion | flops 8606711808 | bytes 20971520 | tf_op jit(solution)/shard_map/dot_general | solution.py:12
  203.5 0.0 reduce-scatter.2.cloned.1.call-update
  203.5 99.5 %reduce-scatter.2.cloned.1.call-done = f32[64,2048]{1,0:T(8,128)} async-done(((f32[1024,2048]{1,0:T(8,128)}), f32[64,2048]{1,0:T(8,128)}) %reduce-scatter.2.cloned.1.call-update) | async-done | bytes 524304 | tf_op jit(solution)/shard_map/reduce_scatter | solution.py:29
  303.0 1.9 slice_multiply_fusion
  (2 shorter events, 0.0 us)
Async XLA Ops:
  7.2 2.3 copy-start
  7.2 64.0 %all-gather.8.cloned.1.call-start = ((), (), s32[]{:S(2)}) async-start(), calls=%async_computation.3 | async-start | bytes 6291456 | tf_op jit(solution)/shard_map/all_gather | solution.py:25
  7.9 125.2 %all-gather.6.cloned.1.call-start = ((), (), s32[]{:S(2)}) async-start(), calls=%async_computation.2 | async-start | bytes 6291456 | tf_op jit(solution)/shard_map/all_gather | solution.py:24
  9.5 29.1 %copy-start.1 = (bf16[2048,256]{1,0:T(8,128)(2,1)S(1)}, bf16[2048,256]{1,0:T(8,128)(2,1)}, u32[]{:S(2)}) copy-start(bf16[2048,256]{1,0:T(8,128)(2,1)} %param.4) | copy-start | bytes 3145732
  36.7 96.4 %copy-start.2 = (f32[2048]{0:T(1024)S(1)}, f32[2048]{0:T(1024)}, u32[]{:S(2)}) copy-start(f32[2048]{0:T(1024)} %param.7) | copy-start | bytes 24580
  38.5 149.8 %all-gather.4.cloned.1.call-start = ((), (), s32[]{:S(2)}) async-start(), calls=%async_computation.1 | async-start | bytes 5242880 | tf_op jit(solution)/shard_map/all_gather | solution.py:22
  39.8 263.2 %reduce-scatter.2.cloned.1.call-start = ((), (), s32[]{:S(2)}) async-start(), calls=%async_computation.4 | async-start | bytes 8912896 | tf_op jit(solution)/shard_map/reduce_scatter | solution.py:29
Sparse Core Ops, SparseCore 0:
  9.7 61.4 all-gather.7
  72.8 60.2 all-gather.5
  134.8 53.4 all-gather.3
  203.6 99.3 reduce-scatter.1
where the time goes:
time: 316 us; the launch traced here: 311 us
  waiting for transfers between devices  243 us (77%)
  blocking collectives  26.9 us (9%)
  matrix products  15.2 us (5%)
  between operations  13.8 us (4%)
  other arithmetic  12.2 us (4%)
    reduce_scatter x1, waiting for transfers between devices, per_device(): lax.psum_scatter(tile_product(row_tile, paired), 'walker', scatter_dimens...  99.5 us
    all_gather x1, waiting for transfers between devices, per_device(): lax.all_gather(col_shard, 'prow', axis=1, tiled=True)  62 us
    all_gather x1, waiting for transfers between devices, per_device(): row_tile = lax.all_gather(row_shard, 'pcol', axis=1, tiled=True)  49.7 us
    all_gather x1, waiting for transfers between devices, per_device(): lax.all_gather(grad_energy, 'prow', axis=1, tiled=True)  31.3 us
    psum x1, blocking collectives, per_device(): lax.psum((column_sums(o_rows), column_sums(o_cols)), 'walker')  26.9 us
    dot_general x1, matrix products, tile_product(): lax.dot_general(row_tile, right_tile, (((0,), (0,)), ((), ())), preferred...  15.2 us
  transfers between devices with their start and end apart: 4, of which 4 were waited for; matrix products, arithmetic and copies ran while one was open for 3% of the time, Pallas kernels for 0%

commit v1 on v0

v1 whole, which is shorter than its diff:
```python
import functools

import jax
import jax.numpy as jnp
from jax import lax
from jax.experimental import pallas as pl
from jax.experimental.pallas import tpu as pltpu
from jax.sharding import PartitionSpec as P

MESH = pl.DeviceIdType.MESH
F32 = jnp.float32
BF16 = jnp.bfloat16

CHUNKS = [
    (0, 0, 0), (0, 0, 1),
    (0, 3, 0), (0, 1, 0), (1, 0, 0),
    (0, 1, 1), (0, 3, 1), (1, 0, 1),
    (0, 2, 0), (0, 2, 1),
    (1, 3, 0), (1, 1, 0), (1, 2, 0),
    (1, 2, 1), (1, 3, 1), (1, 1, 1),
]
LAG = 3


def kernel(
    samples_total,
    r_hbm, c_hbm, g_hbm, e_ref,
    hamil_ref, corr_ref,
    rbuf, cbuf, gbuf, cw, rt, part, csend, crecv, xsend, xown, xrecv, ysend, yrecv,
    mown, mcore, mchip, mrecv, rmean,
    load_sem, rsend_sem, rrecv_sem, msend_sem, mrecv_sem,
    csend_sem, crecv_sem, xsend_sem, xrecv_sem, ysend_sem, yrecv_sem,
):
    w = lax.axis_index("walker")
    p = lax.axis_index("prow")
    q = lax.axis_index("pcol")
    x = w // 4
    yh = lax.rem(w // 2, 2)
    c = lax.rem(w, 2)
    samples, ncols = c_hbm.shape
    width = 2 * ncols

    def device(dx=0, dyh=0, dc=0, dp=0, dz=0):
        xx = lax.rem(x + dx, 4)
        yy = lax.rem(yh + dyh, 2)
        core = lax.rem(c + dc, 2)
        return {
            "walker": (xx * 2 + yy) * 2 + core,
            "prow": lax.rem(p + dp, 2),
            "pcol": lax.rem(q + dz, 4),
        }

    partners = [device(dc=1)]
    partners += [device(dx=a, dyh=b) for a in range(4) for b in range(2) if a or b]
    partners += [device(dp=a, dz=b) for a in range(2) for b in range(4) if a or b]
    partners += [device(dyh=1, dp=1)]
    barrier = pltpu.get_barrier_semaphore()
    for other in partners:
        pl.semaphore_signal(barrier, inc=1, device_id=other, device_id_type=MESH)

    loads = []
    for h in range(2):
        loads.append(pltpu.make_async_copy(
            r_hbm.at[:, pl.ds(128 * h, 128)], rbuf.at[0, 0, h], load_sem.at[h]))
    loads.append(pltpu.make_async_copy(c_hbm, cbuf, load_sem.at[2]))
    loads.append(pltpu.make_async_copy(g_hbm, gbuf, load_sem.at[3]))
    for copy in loads:
        copy.start()
    pl.semaphore_wait(barrier, len(partners))

    started = []

    def send(src, dst, ssem, rsem, target):
        copy = pltpu.make_async_remote_copy(
            src_ref=src, dst_ref=dst, send_sem=ssem, recv_sem=rsem,
            device_id=target, device_id_type=MESH)
        copy.start()
        return copy

    def send_rows(src_slot, dst_slot, number, dp=0, dz=0):
        a, d, h = src_slot
        started.append(send(
            rbuf.at[a, d, h], rbuf.at[dst_slot[0], dst_slot[1], dst_slot[2]],
            rsend_sem.at[number], rrecv_sem.at[dst_slot[0], dst_slot[1], dst_slot[2]],
            device(dp=dp, dz=dz)))

    arrived = set()

    def wait_rows(a, d, h):
        if (a, d, h) in arrived or (a, d) == (0, 0):
            return
        arrived.add((a, d, h))
        pltpu.make_async_remote_copy(
            src_ref=rbuf.at[a, d, h], dst_ref=rbuf.at[a, d, h],
            send_sem=rsend_sem.at[0], recv_sem=rrecv_sem.at[a, d, h],
            device_id=device(dz=1), device_id_type=MESH).wait_recv()

    for h in range(2):
        loads[h].wait()
        send_rows((0, 0, h), (0, 3, h), 3 * h, dz=1)
        send_rows((0, 0, h), (0, 1, h), 3 * h + 1, dz=3)
        send_rows((0, 0, h), (1, 0, h), 3 * h + 2, dp=1)

    mown[...] = jnp.zeros_like(mown)

    def block_sums(ref, lanes):
        def body(i, acc):
            values = ref[pl.ds(pl.multiple_of(i * 128, 128), 128), :].astype(F32)
            return acc + jnp.sum(values.reshape(16, 8, lanes), axis=0)
        acc = lax.fori_loop(0, samples // 128, body, jnp.zeros((8, lanes), F32))
        return jnp.sum(acc, axis=0, keepdims=True)

    for h in range(2):
        mown[h:h + 1, :] = block_sums(rbuf.at[0, 0, h], 128)
    loads[2].wait()
    csum = block_sums(cbuf, ncols)
    for k in range(ncols // 128):
        mown[2 + k:3 + k, :] = csum[:, 128 * k:128 * (k + 1)]

    copy = send(mown, mcore, msend_sem.at[0], mrecv_sem.at[0], device(dc=1))
    copy.wait_recv()
    started.append(copy)
    mchip[0] = mown[...] + mcore[...]
    copies = []
    for dx in range(4):
        for dyh in range(2):
            j = dx * 2 + dyh
            if j:
                copies.append(send(
                    mchip.at[0], mrecv.at[j], msend_sem.at[j], mrecv_sem.at[j], device(dx=dx, dyh=dyh)))
    loads[3].wait()
    total = mchip[0]
    for j, copy in enumerate(copies):
        copy.wait_recv()
        total = total + mrecv[j + 1]
    started += copies
    rmean[0, 0] = total * (1.0 / samples_total)
    mean_copies = []
    for a in range(2):
        for b in range(4):
            if a or b:
                j = 7 + a * 4 + b
                mean_copies.append(send(
                    rmean.at[0, 0], rmean.at[a, (4 - b) % 4],
                    msend_sem.at[j], mrecv_sem.at[j], device(dp=a, dz=b)))

    col_mean = jnp.concatenate([rmean[0, 0, 2 + k:3 + k, :] for k in range(ncols // 128)], axis=1)

    def build(i, _):
        rows = pl.ds(pl.multiple_of(i * 128, 128), 128)
        d_cols = (cbuf[rows, :].astype(F32) - col_mean).astype(BF16)
        cw[rows, pl.ds(0, ncols)] = d_cols
        energy = jnp.broadcast_to(e_ref[pl.ds(i, 1), :], (128, 128)).T
        energy = jnp.concatenate([energy] * (ncols // 128), axis=1)
        weighted = energy * d_cols.astype(F32) + gbuf[rows, :].astype(F32)
        cw[rows, pl.ds(ncols, ncols)] = weighted.astype(BF16)
        return 0

    lax.fori_loop(0, samples // 128, build, 0)

    for copy in mean_copies:
        copy.wait_recv()
    started += mean_copies

    def after_wait(chunk):
        if chunk == (0, 3, 0):
            send_rows((0, 3, 0), (0, 2, 0), 6, dz=1)
        if chunk == (0, 1, 1):
            send_rows((0, 1, 1), (0, 2, 1), 7, dz=3)
        if chunk == (0, 2, 0):
            send_rows((0, 2, 0), (1, 2, 0), 12, dp=1)
        if chunk == (0, 2, 1):
            send_rows((0, 2, 1), (1, 2, 1), 13, dp=1)

    def before(i):
        if i == 6:
            for h in range(2):
                wait_rows(1, 0, h)
                send_rows((1, 0, h), (1, 3, h), 8 + 2 * h, dz=1)
                send_rows((1, 0, h), (1, 1, h), 9 + 2 * h, dz=3)

    core_copies = {}
    half = 64

    def multiply(i):
        chunk = a, d, h = CHUNKS[i]
        wait_rows(a, d, h)
        after_wait(chunk)
        before(i)
        mean = rmean[a, d, h:h + 1, :]

        def center(k, _):
            rows = pl.ds(pl.multiple_of(k * 256, 256), 256)
            values = rbuf[a, d, h, rows, :].astype(F32) - mean
            rt[:, rows] = values.T.astype(BF16)
            return 0

        lax.fori_loop(0, samples // 256, center, 0)

        def product(n, _):
            cols = pl.ds(pl.multiple_of(n * 256, 256), 256)
            tile = jnp.dot(rt[...], cw[:, cols], preferred_element_type=F32)
            part[i % 2, :, cols] = tile
            csend[i, :, cols] = tile.astype(BF16)
            return 0

        lax.fori_loop(0, width // 256, product, 0)
        other = pl.ds(pl.multiple_of(half * (1 - c), half), half)
        core_copies[i] = send(
            csend.at[i, other], crecv.at[i], csend_sem.at[i], crecv_sem.at[i], device(dc=1))
        started.append(core_copies[i])

    def x_target(i):
        return lax.rem(q + CHUNKS[i][1], 4)

    def x_copy(i):
        a, d, h = CHUNKS[i]
        hop = lax.rem(x_target(i) + 4 - x, 4)
        return pltpu.make_async_remote_copy(
            src_ref=xsend.at[i], dst_ref=xrecv.at[2 * a + h, hop - 1],
            send_sem=xsend_sem.at[i], recv_sem=xrecv_sem.at[2 * a + h, hop - 1],
            device_id=device(dx=hop), device_id_type=MESH)

    def chip_sum(i):
        a, d, h = CHUNKS[i]
        core_copies[i].wait_recv()
        mine = pl.ds(pl.multiple_of(half * c, half), half)
        value = part[i % 2, mine, :] + crecv[i].astype(F32)
        away = x_target(i) != x

        @pl.when(away)
        def _():
            xsend[i] = value.astype(BF16)
            x_copy(i).start()

        @pl.when(jnp.logical_not(away))
        def _():
            xown[2 * a + h] = value

    def y_copy(a, h):
        y = 2 * yh + p
        return pltpu.make_async_remote_copy(
            src_ref=ysend.at[2 * a + h], dst_ref=yrecv.at[y],
            send_sem=ysend_sem.at[2 * a + h], recv_sem=yrecv_sem.at[y],
            device_id=device(dyh=h + 2 - yh, dp=a), device_id_type=MESH)

    def x_sum(i):
        a, d, h = CHUNKS[i]
        k = 2 * a + h

        @pl.when(x_target(i) == x)
        def _():
            value = xown[k]
            for hop in range(3):
                pltpu.make_async_remote_copy(
                    src_ref=xsend.at[i], dst_ref=xrecv.at[k, hop],
                    send_sem=xsend_sem.at[i], recv_sem=xrecv_sem.at[k, hop],
                    device_id=device(dx=1), device_id_type=MESH).wait_recv()
                value = value + xrecv[k, hop].astype(F32)
            if a == 0:
                @pl.when(yh == h)
                def _():
                    yrecv[2 * yh + p] = value.astype(BF16)

                @pl.when(yh != h)
                def _():
                    ysend[k] = value.astype(BF16)
                    y_copy(a, h).start()
            else:
                ysend[k] = value.astype(BF16)
                y_copy(a, h).start()

    count = len(CHUNKS)
    for i in range(count + LAG):
        if i < count:
            multiply(i)
        if 1 <= i <= count:
            chip_sum(i - 1)
        if i >= LAG:
            x_sum(i - LAG)

    for source in range(4):
        @pl.when(source != 2 * yh + p)
        def _():
            pltpu.make_async_remote_copy(
                src_ref=ysend.at[0], dst_ref=yrecv.at[source],
                send_sem=ysend_sem.at[0], recv_sem=yrecv_sem.at[source],
                device_id=device(dp=1), device_id_type=MESH).wait_recv()
    for part_p in range(2):
        value = yrecv[part_p].astype(F32) + yrecv[2 + part_p].astype(F32)
        cols = pl.ds(part_p * ncols, ncols)
        corr_ref[:, cols] = value[:, :ncols]
        hamil_ref[:, cols] = value[:, ncols:]

    for copy in started:
        copy.wait_send()
    for i in range(count):
        @pl.when(x_target(i) != x)
        def _(i=i):
            x_copy(i).wait_send()
    for a in range(2):
        for h in range(2):
            if a:
                y_copy(a, h).wait_send()
            else:
                @pl.when(yh != h)
                def _(a=a, h=h):
                    y_copy(a, h).wait_send()


def per_device(o_rows, o_cols, grad_energy, energy):
    samples, nrows = o_rows.shape
    ncols = o_cols.shape[1]
    width = 2 * ncols
    total = samples * lax.axis_size("walker")
    dma = pltpu.SemaphoreType.DMA
    out = jax.ShapeDtypeStruct((64, width), F32)
    hamil, corr = pl.pallas_call(
        functools.partial(kernel, total),
        name="tiles",
        out_shape=(out, out),
        in_specs=[pl.BlockSpec(memory_space=pl.ANY)] * 3 + [pl.BlockSpec(memory_space=pltpu.VMEM)],
        out_specs=(pl.BlockSpec(memory_space=pltpu.VMEM),) * 2,
        scratch_shapes=[
            pltpu.VMEM((2, 4, 2, samples, 128), BF16),
            pltpu.VMEM((samples, ncols), BF16),
            pltpu.VMEM((samples, ncols), BF16),
            pltpu.VMEM((samples, width), BF16),
            pltpu.VMEM((128, samples), BF16),
            pltpu.VMEM((2, 128, width), F32),
            pltpu.VMEM((16, 128, width), BF16),
            pltpu.VMEM((16, 64, width), BF16),
            pltpu.VMEM((16, 64, width), BF16),
            pltpu.VMEM((4, 64, width), F32),
            pltpu.VMEM((4, 3, 64, width), BF16),
            pltpu.VMEM((4, 64, width), BF16),
            pltpu.VMEM((4, 64, width), BF16),
            pltpu.VMEM((8, 128), F32),
            pltpu.VMEM((8, 128), F32),
            pltpu.VMEM((1, 8, 128), F32),
            pltpu.VMEM((8, 8, 128), F32),
            pltpu.VMEM((2, 4, 8, 128), F32),
            dma((4,)), dma((14,)), dma((2, 4, 2)), dma((15,)), dma((15,)),
            dma((16,)), dma((16,)), dma((16,)), dma((4, 3)), dma((4,)), dma((4,)),
        ],
        compiler_params=pltpu.CompilerParams(
            collective_id=0, has_side_effects=True, vmem_limit_bytes=56 * 2**20),
        cost_estimate=pl.CostEstimate(
            flops=2 * samples * 2048 * width, bytes_accessed=6 * 2**20, transcendentals=0),
    )(o_rows, o_cols, grad_energy, energy.reshape(samples // 128, 128))
    scale = 1.0 / total
    return hamil * scale, corr * scale


def solution(mesh):
    in_specs = (
        P("walker", ("prow", "pcol")),
        P("walker", ("pcol", "prow")),
        P("walker", ("pcol", "prow")),
        P("walker"),
    )
    out_specs = (P(("prow", "walker"), "pcol"), P(("prow", "walker"), "pcol"))
    return jax.shard_map(
        per_device, mesh=mesh, in_specs=in_specs, out_specs=out_specs, check_vma=False
    )
```

time: 316 us -> 111 us (0.35)
  the two profiles are of different devices: /device:TPU:20 before, /device:TPU:26 now
where the time goes in v1:
time: 111 us
  Pallas kernels  108 us (97%)
  other arithmetic  1.86 us (2%)
    pallas_call x1, Pallas kernels, per_device(): pl.pallas_call(functools.partial(kernel, total), name='tiles', out_shape=...  108 us

profile of v1, /device:TPU:26, one launch (start us, length us, event | category | flops | bytes accessed | tf_op | source)
XLA Modules:
  0.0 110.7 jit_solution(7516866642585202704)
XLA Ops:
  0.6 108.2 %tiles.1 = (f32[64,1024]{1,0:T(8,128)}, f32[64,1024]{1,0:T(8,128)}) custom-call(bf16[2048,256]{1,0:T(8,128)(2,1)} %r_hbm.1, bf16[2048,512]{1,0:T(8,128)(2,1)} %c_hbm.1, bf16[2048,512]{1,0:T(8,128)(2,1)} %g_hbm.1, f32[16,128]{1,0:T(8,128)} %bitcast.1), custom_call_target="tpu_custom_call" | custom-call | flops 8589934592 | bytes 6291456 | tf_op jit(solution)/shard_map/tiles/pallas_call | solution.py:318
  108.8 1.9 %broadcast_multiply_fusion = (f32[64,1024]{1,0:T(8,128)}, f32[64,1024]{1,0:T(8,128)}) fusion(f32[64,1024]{1,0:T(8,128)} %get-tuple-element.5, f32[64,1024]{1,0:T(8,128)} %get-tuple-element.4), kind=kLoop, calls=%fused_computation | loop fusion | flops 131072 | bytes 1048576 | tf_op jit(solution)/shard_map/mul | solution.py:352

commit v2 on v1

v2 whole, which is shorter than its diff:
```python
import functools

import jax
import jax.numpy as jnp
from jax import lax
from jax.experimental import pallas as pl
from jax.experimental.pallas import tpu as pltpu
from jax.sharding import PartitionSpec as P

MESH = pl.DeviceIdType.MESH
F32 = jnp.float32
BF16 = jnp.bfloat16

GROUPS = [
    [(0, 0, 0), (0, 0, 1)],
    [(0, 3, 0), (0, 1, 1), (1, 0, 0)],
    [(0, 3, 1), (0, 1, 0), (1, 0, 1)],
    [(0, 2, 0), (0, 2, 1)],
    [(1, 3, 0), (1, 1, 0), (1, 2, 0)],
    [(1, 3, 1), (1, 2, 1), (1, 1, 1)],
]
CHUNKS = [chunk for group in GROUPS for chunk in group]
SLOT = {chunk: i for i, chunk in enumerate(CHUNKS)}


def kernel(
    samples_total,
    r_hbm, c_hbm, g_hbm, e_ref,
    hamil_ref, corr_ref,
    rbuf, cbuf, gbuf, cw, rt, part, csend, crecv, xsend, xown, xrecv, ysend, yrecv,
    mown, mcore, mchip, mrecv, rmean, cmean,
    load_sem, rsend_sem, rrecv_sem, msend_sem, mrecv_sem,
    csend_sem, crecv_sem, xsend_sem, xrecv_sem, ysend_sem, yrecv_sem,
):
    w = lax.axis_index("walker")
    p = lax.axis_index("prow")
    q = lax.axis_index("pcol")
    x = w // 4
    yh = lax.rem(w // 2, 2)
    c = lax.rem(w, 2)
    samples, ncols = c_hbm.shape
    width = 2 * ncols

    def device(dx=0, dyh=0, dc=0, dp=0, dz=0):
        xx = lax.rem(x + dx, 4)
        yy = lax.rem(yh + dyh, 2)
        core = lax.rem(c + dc, 2)
        return {
            "walker": (xx * 2 + yy) * 2 + core,
            "prow": lax.rem(p + dp, 2),
            "pcol": lax.rem(q + dz, 4),
        }

    partners = [device(dc=1)]
    partners += [device(dx=a, dyh=b) for a in range(4) for b in range(2) if a or b]
    partners += [device(dp=a, dz=b) for a in range(2) for b in range(4) if a or b]
    partners += [device(dyh=1, dp=1)]
    barrier = pltpu.get_barrier_semaphore()
    for other in partners:
        pl.semaphore_signal(barrier, inc=1, device_id=other, device_id_type=MESH)

    loads = []
    for h in range(2):
        loads.append(pltpu.make_async_copy(
            r_hbm.at[:, pl.ds(128 * h, 128)], rbuf.at[h], load_sem.at[h]))
    loads.append(pltpu.make_async_copy(c_hbm, cbuf, load_sem.at[2]))
    loads.append(pltpu.make_async_copy(g_hbm, gbuf, load_sem.at[3]))
    for copy in loads:
        copy.start()
    pl.semaphore_wait(barrier, len(partners))

    started = []

    def send(src, dst, ssem, rsem, target):
        copy = pltpu.make_async_remote_copy(
            src_ref=src, dst_ref=dst, send_sem=ssem, recv_sem=rsem,
            device_id=target, device_id_type=MESH)
        copy.start()
        return copy

    piece = samples // 2

    def rows_of(i, k):
        return rbuf.at[i, pl.ds(piece * k, piece)]

    def send_rows(source, target, ks=(0, 1), dp=0, dz=0):
        i = SLOT[target]
        for k in ks:
            number = len(row_copies)
            if source is None:
                src = r_hbm.at[pl.ds(piece * k, piece), pl.ds(128 * target[2], 128)]
            else:
                src = rows_of(SLOT[source], k)
            row_copies.append(send(
                src, rows_of(i, k), rsend_sem.at[number], rrecv_sem.at[i, k], device(dp=dp, dz=dz)))

    row_copies = []

    def wait_piece(i, k):
        pltpu.make_async_remote_copy(
            src_ref=rows_of(i, k), dst_ref=rows_of(i, k), send_sem=rsend_sem.at[0], recv_sem=rrecv_sem.at[i, k],
            device_id=device(dz=1), device_id_type=MESH).wait_recv()

    waited = set()

    def wait_rows(*chunks, ks=(0, 1)):
        for chunk in chunks:
            for k in ks:
                if (chunk, k) not in waited:
                    waited.add((chunk, k))
                    wait_piece(SLOT[chunk], k)

    def send_own(up, down, across):
        for k in range(2):
            send_rows(None, (0, 3, up), (k,), dz=1)
            send_rows(None, (0, 1, down), (k,), dz=3)
            send_rows(None, (1, 0, across), (k,), dp=1)

    send_own(0, 1, 0)
    loads[0].wait()
    loads[1].wait()

    mown[...] = jnp.zeros_like(mown)

    def block_sums(ref, lanes):
        def body(i, acc):
            values = ref[pl.ds(pl.multiple_of(i * 128, 128), 128), :].astype(F32)
            return acc + jnp.sum(values.reshape(16, 8, lanes), axis=0)
        acc = lax.fori_loop(0, samples // 128, body, jnp.zeros((8, lanes), F32))
        return jnp.sum(acc, axis=0, keepdims=True)

    for h in range(2):
        mown[h:h + 1, :] = block_sums(rbuf.at[h], 128)
    loads[2].wait()
    csum = block_sums(cbuf, ncols)
    for k in range(ncols // 128):
        mown[2 + k:3 + k, :] = csum[:, 128 * k:128 * (k + 1)]

    copy = send(mown, mcore, msend_sem.at[0], mrecv_sem.at[0], device(dc=1))
    copy.wait_recv()
    started.append(copy)
    mchip[0] = mown[...] + mcore[...]
    copies = []
    for dx in range(4):
        for dyh in range(2):
            j = dx * 2 + dyh
            if j:
                copies.append(send(
                    mchip.at[0], mrecv.at[j], msend_sem.at[j], mrecv_sem.at[j], device(dx=dx, dyh=dyh)))
    send_own(1, 0, 1)
    loads[3].wait()
    total = mchip[0]
    for j, copy in enumerate(copies):
        copy.wait_recv()
        total = total + mrecv[j + 1]
    started += copies
    rmean[0, 0] = total * (1.0 / samples_total)
    mean_copies = []
    for a in range(2):
        for b in range(4):
            if a or b:
                j = 7 + a * 4 + b
                mean_copies.append(send(
                    rmean.at[0, 0], rmean.at[a, (4 - b) % 4],
                    msend_sem.at[j], mrecv_sem.at[j], device(dp=a, dz=b)))

    col_mean = jnp.concatenate([rmean[0, 0, 2 + k:3 + k, :] for k in range(ncols // 128)], axis=1)

    def build(i, _):
        rows = pl.ds(pl.multiple_of(i * 128, 128), 128)
        d_cols = (cbuf[rows, :].astype(F32) - col_mean).astype(BF16)
        cw[rows, pl.ds(0, ncols)] = d_cols
        energy = jnp.broadcast_to(e_ref[pl.ds(i, 1), :], (128, 128)).T
        energy = jnp.concatenate([energy] * (ncols // 128), axis=1)
        weighted = energy * d_cols.astype(F32) + gbuf[rows, :].astype(F32)
        cw[rows, pl.ds(ncols, ncols)] = weighted.astype(BF16)
        return 0

    lax.fori_loop(0, samples // 128, build, 0)

    half = 64
    mine = pl.ds(pl.multiple_of(half * c, half), half)
    other = pl.ds(pl.multiple_of(half * (1 - c), half), half)
    part_cols = [pl.ds(ncols * n, ncols) for n in range(2)]

    def core_copy(i, n):
        return pltpu.make_async_remote_copy(
            src_ref=csend.at[i, n], dst_ref=crecv.at[i, n], send_sem=csend_sem.at[i, n],
            recv_sem=crecv_sem.at[i, n], device_id=device(dc=1), device_id_type=MESH)

    def center(i):
        mean = cmean[i, 0:1, :]

        def body(k, _):
            rows = pl.ds(pl.multiple_of(k * 256, 256), 256)
            rt[rows, :] = (rbuf[i, rows, :].astype(F32) - mean).astype(BF16)
            return 0

        lax.fori_loop(0, samples // 256, body, 0)

    def product(cols):
        return lax.dot_general(
            rt[...], cw[:, cols], (((0,), (0,)), ((), ())), preferred_element_type=F32)

    def to_other_core(i, n):
        csend[i, n] = part[i, other, part_cols[n]].astype(BF16)
        core_copy(i, n).start()

    def multiply(i):
        center(i)
        part[i] = product(pl.ds(0, width))
        for n in range(2):
            to_other_core(i, n)

    def multiply_in_parts(i):
        center(i)
        for n in range(2):
            part[i, :, part_cols[n]] = product(part_cols[n])
            to_other_core(i, n)

    def multiply_group(group):
        first = SLOT[GROUPS[group][0]]

        def body(i, _):
            multiply(i)
            return 0

        lax.fori_loop(first, first + len(GROUPS[group]), body, 0)

    def x_target(i):
        return lax.rem(q + CHUNKS[i][1], 4)

    def x_copy(i, n):
        a, d, h = CHUNKS[i]
        hop = lax.rem(x_target(i) + 4 - x, 4)
        return pltpu.make_async_remote_copy(
            src_ref=xsend.at[i, n], dst_ref=xrecv.at[2 * a + h, hop - 1, n],
            send_sem=xsend_sem.at[i, n], recv_sem=xrecv_sem.at[2 * a + h, hop - 1, n],
            device_id=device(dx=hop), device_id_type=MESH)

    def chip_sum(i):
        a, d, h = CHUNKS[i]
        away = x_target(i) != x
        for n in range(2):
            core_copy(i, n).wait_recv()
            value = part[i, mine, part_cols[n]] + crecv[i, n].astype(F32)

            @pl.when(away)
            def _():
                xsend[i, n] = value.astype(BF16)
                x_copy(i, n).start()

            @pl.when(jnp.logical_not(away))
            def _():
                xown[2 * a + h, n] = value

    def y_copy(a, h, n):
        y = 2 * yh + p
        return pltpu.make_async_remote_copy(
            src_ref=ysend.at[2 * a + h, n], dst_ref=yrecv.at[y, n],
            send_sem=ysend_sem.at[2 * a + h, n], recv_sem=yrecv_sem.at[y, n],
            device_id=device(dyh=h + 2 - yh, dp=a), device_id_type=MESH)

    def x_sum(i):
        a, d, h = CHUNKS[i]
        row = 2 * a + h

        @pl.when(x_target(i) == x)
        def _():
            for n in range(2):
                value = xown[row, n]
                for hop in range(3):
                    pltpu.make_async_remote_copy(
                        src_ref=xsend.at[i, n], dst_ref=xrecv.at[row, hop, n],
                        send_sem=xsend_sem.at[i, n], recv_sem=xrecv_sem.at[row, hop, n],
                        device_id=device(dx=1), device_id_type=MESH).wait_recv()
                    value = value + xrecv[row, hop, n].astype(F32)
                if a == 0:
                    @pl.when(yh == h)
                    def _():
                        yrecv[2 * yh + p, n] = value.astype(BF16)

                    @pl.when(yh != h)
                    def _():
                        ysend[row, n] = value.astype(BF16)
                        y_copy(a, h, n).start()
                else:
                    ysend[row, n] = value.astype(BF16)
                    y_copy(a, h, n).start()

    def chip_sums(group):
        for chunk in GROUPS[group]:
            chip_sum(SLOT[chunk])

    def x_sums(group):
        for chunk in GROUPS[group]:
            x_sum(SLOT[chunk])

    count = len(CHUNKS)
    for h in range(2):
        cmean[SLOT[0, 0, h], 0:1, :] = rmean[0, 0, h:h + 1, :]
    multiply_group(0)
    for k in range(2):
        wait_rows((0, 3, 0), (0, 1, 1), ks=(k,))
        send_rows((0, 3, 0), (0, 2, 0), (k,), dz=1)
        send_rows((0, 1, 1), (0, 2, 1), (k,), dz=3)
    send_rows((0, 3, 0), (1, 3, 0), (1,), dp=1)
    wait_rows((1, 0, 0))
    send_rows((1, 0, 0), (1, 3, 0), (0,), dz=1)
    send_rows((1, 0, 0), (1, 1, 0), dz=3)
    chip_sums(0)
    for copy in mean_copies:
        copy.wait_recv()
    started += mean_copies
    for i, (a, d, h) in enumerate(CHUNKS):
        if (a, d) != (0, 0):
            cmean[i, 0:1, :] = rmean[a, d, h:h + 1, :]
    multiply_group(1)
    chip_sums(1)
    x_sums(0)
    wait_rows((1, 0, 1))
    send_rows((1, 0, 1), (1, 3, 1), dz=1)
    send_rows((1, 0, 1), (1, 1, 1), dz=3)
    wait_rows((0, 3, 1), (0, 1, 0))
    multiply_group(2)
    for k in range(2):
        for h in range(2):
            wait_rows((0, 2, h), ks=(k,))
            send_rows((0, 2, h), (1, 2, h), (k,), dp=1)
        if k == 0:
            chip_sums(2)
            x_sums(1)
    multiply_group(3)
    x_sums(2)
    chip_sums(3)
    for j, chunk in enumerate(GROUPS[4]):
        wait_rows(chunk)
        multiply(SLOT[chunk])
        if j == 1:
            x_sums(3)
        if j:
            chip_sum(SLOT[GROUPS[4][j - 1]])
    chip_sum(SLOT[GROUPS[4][2]])
    for chunk in GROUPS[5][:2]:
        wait_rows(chunk)
        multiply(SLOT[chunk])
    for chunk in GROUPS[5][:2]:
        chip_sum(SLOT[chunk])
    x_sums(4)
    wait_rows(GROUPS[5][2])
    multiply_in_parts(SLOT[GROUPS[5][2]])
    chip_sum(SLOT[GROUPS[5][2]])
    x_sums(5)

    for n, out in enumerate((corr_ref, hamil_ref)):
        for source in range(4):
            @pl.when(source != 2 * yh + p)
            def _(source=source, n=n):
                pltpu.make_async_remote_copy(
                    src_ref=ysend.at[0, n], dst_ref=yrecv.at[source, n],
                    send_sem=ysend_sem.at[0, n], recv_sem=yrecv_sem.at[source, n],
                    device_id=device(dp=1), device_id_type=MESH).wait_recv()
        for part_p in range(2):
            value = yrecv[part_p, n].astype(F32) + yrecv[2 + part_p, n].astype(F32)
            out[:, part_cols[part_p]] = value

    for copy in started + row_copies:
        copy.wait_send()
    for n in range(2):
        for i in range(count):
            core_copy(i, n).wait_send()

            @pl.when(x_target(i) != x)
            def _(i=i, n=n):
                x_copy(i, n).wait_send()
        for h in range(2):
            y_copy(1, h, n).wait_send()

            @pl.when(yh != h)
            def _(h=h, n=n):
                y_copy(0, h, n).wait_send()


def per_device(o_rows, o_cols, grad_energy, energy):
    samples, nrows = o_rows.shape
    ncols = o_cols.shape[1]
    width = 2 * ncols
    total = samples * lax.axis_size("walker")
    dma = pltpu.SemaphoreType.DMA
    out = jax.ShapeDtypeStruct((64, width), F32)
    hamil, corr = pl.pallas_call(
        functools.partial(kernel, total),
        name="tiles",
        out_shape=(out, out),
        in_specs=[pl.BlockSpec(memory_space=pl.ANY)] * 3 + [pl.BlockSpec(memory_space=pltpu.VMEM)],
        out_specs=(pl.BlockSpec(memory_space=pltpu.VMEM),) * 2,
        scratch_shapes=[
            pltpu.VMEM((16, samples, 128), BF16),
            pltpu.VMEM((samples, ncols), BF16),
            pltpu.VMEM((samples, ncols), BF16),
            pltpu.VMEM((samples, width), BF16),
            pltpu.VMEM((samples, 128), BF16),
            pltpu.VMEM((16, 128, width), F32),
            pltpu.VMEM((16, 2, 64, ncols), BF16),
            pltpu.VMEM((16, 2, 64, ncols), BF16),
            pltpu.VMEM((16, 2, 64, ncols), BF16),
            pltpu.VMEM((4, 2, 64, ncols), F32),
            pltpu.VMEM((4, 3, 2, 64, ncols), BF16),
            pltpu.VMEM((4, 2, 64, ncols), BF16),
            pltpu.VMEM((4, 2, 64, ncols), BF16),
            pltpu.VMEM((8, 128), F32),
            pltpu.VMEM((8, 128), F32),
            pltpu.VMEM((1, 8, 128), F32),
            pltpu.VMEM((8, 8, 128), F32),
            pltpu.VMEM((2, 4, 8, 128), F32),
            pltpu.VMEM((16, 8, 128), F32),
            dma((4,)), dma((28,)), dma((16, 2)), dma((15,)), dma((15,)),
            dma((16, 2)), dma((16, 2)), dma((16, 2)), dma((4, 3, 2)), dma((4, 2)), dma((4, 2)),
        ],
        compiler_params=pltpu.CompilerParams(
            collective_id=0, has_side_effects=True, vmem_limit_bytes=56 * 2**20),
        cost_estimate=pl.CostEstimate(
            flops=2 * samples * 2048 * width, bytes_accessed=6 * 2**20, transcendentals=0),
    )(o_rows, o_cols, grad_energy, energy.reshape(samples // 128, 128))
    scale = 1.0 / total
    return hamil * scale, corr * scale


def solution(mesh):
    in_specs = (
        P("walker", ("prow", "pcol")),
        P("walker", ("pcol", "prow")),
        P("walker", ("pcol", "prow")),
        P("walker"),
    )
    out_specs = (P(("prow", "walker"), "pcol"), P(("prow", "walker"), "pcol"))
    return jax.shard_map(
        per_device, mesh=mesh, in_specs=in_specs, out_specs=out_specs, check_vma=False
    )
```

time: 111 us -> 88.1 us (0.79)
  the two profiles are of different devices: /device:TPU:26 before, /device:TPU:20 now
where the time goes in v2:
time: 88.1 us; the launch traced here: 86.4 us
  Pallas kernels  83.9 us (95%)
  other arithmetic  1.86 us (2%)
    pallas_call x1, Pallas kernels, per_device(): pl.pallas_call(functools.partial(kernel, total), name='tiles', out_shape=...  83.9 us
    mul x1, other arithmetic, per_device(): return (hamil * scale, corr * scale)  1.86 us

profile of v2, /device:TPU:20, one launch (start us, length us, event | category | flops | bytes accessed | tf_op | source)
XLA Modules:
  0.0 86.4 jit_solution(4641189623858440990)
XLA Ops:
  0.6 83.9 %tiles.1 = (f32[64,1024]{1,0:T(8,128)}, f32[64,1024]{1,0:T(8,128)}) custom-call(bf16[2048,256]{1,0:T(8,128)(2,1)} %r_hbm.1, bf16[2048,512]{1,0:T(8,128)(2,1)} %c_hbm.1, bf16[2048,512]{1,0:T(8,128)(2,1)} %g_hbm.1, f32[16,128]{1,0:T(8,128)} %bitcast.1), custom_call_target="tpu_custom_call" | custom-call | flops 8589934592 | bytes 6291456 | tf_op jit(solution)/shard_map/tiles/pallas_call | solution.py:391
  84.5 1.9 %broadcast_multiply_fusion = (f32[64,1024]{1,0:T(8,128)}, f32[64,1024]{1,0:T(8,128)}) fusion(f32[64,1024]{1,0:T(8,128)} %get-tuple-element.5, f32[64,1024]{1,0:T(8,128)} %get-tuple-element.4), kind=kLoop, calls=%fused_computation | loop fusion | flops 131072 | bytes 1048576 | tf_op jit(solution)/shard_map/mul | solution.py:426

commit v3 on v2

--- a/solution.py
+++ b/solution.py
@@ -16,11 +16,16 @@
     [(0, 3, 0), (0, 1, 1), (1, 0, 0)],
     [(0, 3, 1), (0, 1, 0), (1, 0, 1)],
     [(0, 2, 0), (0, 2, 1)],
-    [(1, 3, 0), (1, 1, 0), (1, 2, 0)],
-    [(1, 3, 1), (1, 2, 1), (1, 1, 1)],
+    [(1, 3, 0), (1, 1, 0)],
+    [(1, 2, 0), (1, 3, 1), (1, 1, 1), (1, 2, 1)],
 ]
 CHUNKS = [chunk for group in GROUPS for chunk in group]
 SLOT = {chunk: i for i, chunk in enumerate(CHUNKS)}
+HALVES = (0, 64, 128)
+CUTS = {chunk: HALVES for chunk in CHUNKS}
+CUTS[1, 3, 0] = CUTS[1, 1, 0] = (0, 43, 128)
+CUTS[1, 3, 1] = CUTS[1, 1, 1] = (0, 86, 128)
+CUTS[1, 2, 1] = (0, 43, 86, 128)
 
 
 def kernel(
@@ -78,45 +83,46 @@
         copy.start()
         return copy
 
-    piece = samples // 2
-
-    def rows_of(i, k):
-        return rbuf.at[i, pl.ds(piece * k, piece)]
-
-    def send_rows(source, target, ks=(0, 1), dp=0, dz=0):
+    def span(chunk, k):
+        unit = samples // 128
+        low, high = CUTS[chunk][k], CUTS[chunk][k + 1]
+        return pl.ds(low * unit, (high - low) * unit)
+
+    def pieces(chunk):
+        return range(len(CUTS[chunk]) - 1)
+
+    def send_rows(source, target, ks=None, dp=0, dz=0):
         i = SLOT[target]
-        for k in ks:
+        for k in pieces(target) if ks is None else ks:
             number = len(row_copies)
+            rows = span(target, k)
             if source is None:
-                src = r_hbm.at[pl.ds(piece * k, piece), pl.ds(128 * target[2], 128)]
+                src = r_hbm.at[rows, pl.ds(128 * target[2], 128)]
             else:
-                src = rows_of(SLOT[source], k)
+                src = rbuf.at[SLOT[source], rows]
             row_copies.append(send(
-                src, rows_of(i, k), rsend_sem.at[number], rrecv_sem.at[i, k], device(dp=dp, dz=dz)))
+                src, rbuf.at[i, rows], rsend_sem.at[number], rrecv_sem.at[i, k], device(dp=dp, dz=dz)))
 
     row_copies = []
 
-    def wait_piece(i, k):
-        pltpu.make_async_remote_copy(
-            src_ref=rows_of(i, k), dst_ref=rows_of(i, k), send_sem=rsend_sem.at[0], recv_sem=rrecv_sem.at[i, k],
-            device_id=device(dz=1), device_id_type=MESH).wait_recv()
-
     waited = set()
 
-    def wait_rows(*chunks, ks=(0, 1)):
+    def wait_rows(*chunks, ks=None):
         for chunk in chunks:
-            for k in ks:
+            for k in pieces(chunk) if ks is None else ks:
                 if (chunk, k) not in waited:
                     waited.add((chunk, k))
-                    wait_piece(SLOT[chunk], k)
-
-    def send_own(up, down, across):
+                    rows = rbuf.at[SLOT[chunk], span(chunk, k)]
+                    pltpu.make_async_remote_copy(
+                        src_ref=rows, dst_ref=rows, send_sem=rsend_sem.at[0], recv_sem=rrecv_sem.at[SLOT[chunk], k],
+                        device_id=device(dz=1), device_id_type=MESH).wait_recv()
+
+    for h in range(2):
         for k in range(2):
-            send_rows(None, (0, 3, up), (k,), dz=1)
-            send_rows(None, (0, 1, down), (k,), dz=3)
-            send_rows(None, (1, 0, across), (k,), dp=1)
-
-    send_own(0, 1, 0)
+            send_rows(None, (0, 3, h), (k,), dz=1)
+            send_rows(None, (0, 1, 1 - h), (k,), dz=3)
+            if h == 0:
+                send_rows(None, (1, 0, 0), (k,), dp=1)
     loads[0].wait()
     loads[1].wait()
 
@@ -147,7 +153,7 @@
             if j:
                 copies.append(send(
                     mchip.at[0], mrecv.at[j], msend_sem.at[j], mrecv_sem.at[j], device(dx=dx, dyh=dyh)))
-    send_own(1, 0, 1)
+    send_rows(None, (1, 0, 1), dp=1)
     loads[3].wait()
     total = mchip[0]
     for j, copy in enumerate(copies):
@@ -188,19 +194,16 @@
             src_ref=csend.at[i, n], dst_ref=crecv.at[i, n], send_sem=csend_sem.at[i, n],
             recv_sem=crecv_sem.at[i, n], device_id=device(dc=1), device_id_type=MESH)
 
-    def center(i):
+    def center(i, first=0, last=16):
         mean = cmean[i, 0:1, :]
+        step = samples // 16
 
         def body(k, _):
-            rows = pl.ds(pl.multiple_of(k * 256, 256), 256)
+            rows = pl.ds(pl.multiple_of(k * step, step), step)
             rt[rows, :] = (rbuf[i, rows, :].astype(F32) - mean).astype(BF16)
             return 0
 
-        lax.fori_loop(0, samples // 256, body, 0)
-
-    def product(cols):
-        return lax.dot_general(
-            rt[...], cw[:, cols], (((0,), (0,)), ((), ())), preferred_element_type=F32)
+        lax.fori_loop(first, last, body, 0)
 
     def to_other_core(i, n):
         csend[i, n] = part[i, other, part_cols[n]].astype(BF16)
@@ -208,15 +211,18 @@
 
     def multiply(i):
         center(i)
-        part[i] = product(pl.ds(0, width))
+        part[i] = lax.dot_general(
+            rt[...], cw[...], (((0,), (0,)), ((), ())), preferred_element_type=F32)
         for n in range(2):
             to_other_core(i, n)
 
-    def multiply_in_parts(i):
-        center(i)
-        for n in range(2):
-            part[i, :, part_cols[n]] = product(part_cols[n])
-            to_other_core(i, n)
+    def multiply_piece(chunk, k, first):
+        i = SLOT[chunk]
+        rows = span(chunk, k)
+        values = (rbuf[i, rows, :].astype(F32) - cmean[i, 0:1, :]).astype(BF16)
+        tile = lax.dot_general(
+            values, cw[rows, :], (((0,), (0,)), ((), ())), preferred_element_type=F32)
+        part[i] = tile if first else part[i] + tile
 
     def multiply_group(group):
         first = SLOT[GROUPS[group][0]]
@@ -307,7 +313,7 @@
     send_rows((0, 3, 0), (1, 3, 0), (1,), dp=1)
     wait_rows((1, 0, 0))
     send_rows((1, 0, 0), (1, 3, 0), (0,), dz=1)
-    send_rows((1, 0, 0), (1, 1, 0), dz=3)
+    send_rows((1, 0, 0), (1, 1, 0), (0,), dz=3)
     chip_sums(0)
     for copy in mean_copies:
         copy.wait_recv()
@@ -322,34 +328,47 @@
     send_rows((1, 0, 1), (1, 3, 1), dz=1)
     send_rows((1, 0, 1), (1, 1, 1), dz=3)
     wait_rows((0, 3, 1), (0, 1, 0))
+    send_rows((0, 1, 0), (1, 1, 0), (1,), dp=1)
     multiply_group(2)
-    for k in range(2):
-        for h in range(2):
-            wait_rows((0, 2, h), ks=(k,))
-            send_rows((0, 2, h), (1, 2, h), (k,), dp=1)
-        if k == 0:
-            chip_sums(2)
-            x_sums(1)
+    wait_rows((0, 2, 0), ks=(0,))
+    send_rows((0, 2, 0), (1, 2, 0), (0,), dp=1)
+    chip_sums(2)
+    x_sums(1)
+    wait_rows((0, 2, 0), (0, 2, 1))
+    send_rows((0, 2, 0), (1, 2, 0), (1,), dp=1)
+    send_rows((0, 2, 1), (1, 2, 1), (2,), dp=1)
     multiply_group(3)
     x_sums(2)
     chip_sums(3)
-    for j, chunk in enumerate(GROUPS[4]):
+    for chunk in GROUPS[4]:
         wait_rows(chunk)
         multiply(SLOT[chunk])
-        if j == 1:
-            x_sums(3)
-        if j:
-            chip_sum(SLOT[GROUPS[4][j - 1]])
-    chip_sum(SLOT[GROUPS[4][2]])
-    for chunk in GROUPS[5][:2]:
+    chip_sums(4)
+    wait_rows((1, 3, 1), ks=(0,))
+    send_rows((1, 3, 1), (1, 2, 1), (0,), dz=1)
+    wait_rows((1, 1, 1), ks=(0,))
+    send_rows((1, 1, 1), (1, 2, 1), (1,), dz=3)
+    multiply_piece((1, 3, 1), 0, True)
+    multiply_piece((1, 1, 1), 0, True)
+    x_sums(3)
+    for chunk in GROUPS[5][:3]:
         wait_rows(chunk)
-        multiply(SLOT[chunk])
-    for chunk in GROUPS[5][:2]:
+        if chunk == (1, 2, 0):
+            multiply(SLOT[chunk])
+        else:
+            multiply_piece(chunk, 1, False)
+            for n in range(2):
+                to_other_core(SLOT[chunk], n)
+    for chunk in GROUPS[5][:3]:
         chip_sum(SLOT[chunk])
+    last = (1, 2, 1)
+    for k in (2, 0, 1):
+        wait_rows(last, ks=(k,))
+        multiply_piece(last, k, k == 2)
+    for n in range(2):
+        to_other_core(SLOT[last], n)
     x_sums(4)
-    wait_rows(GROUPS[5][2])
-    multiply_in_parts(SLOT[GROUPS[5][2]])
-    chip_sum(SLOT[GROUPS[5][2]])
+    chip_sum(SLOT[last])
     x_sums(5)
 
     for n, out in enumerate((corr_ref, hamil_ref)):
@@ -414,7 +433,7 @@
             pltpu.VMEM((8, 8, 128), F32),
             pltpu.VMEM((2, 4, 8, 128), F32),
             pltpu.VMEM((16, 8, 128), F32),
-            dma((4,)), dma((28,)), dma((16, 2)), dma((15,)), dma((15,)),
+            dma((4,)), dma((30,)), dma((16, 3)), dma((15,)), dma((15,)),
             dma((16, 2)), dma((16, 2)), dma((16, 2)), dma((4, 3, 2)), dma((4, 2)), dma((4, 2)),
         ],
         compiler_params=pltpu.CompilerParams(

time: 88.1 us -> 86.7 us (0.984); the launches traced: 86.4 us -> 86.6 us
  no operation moved by 1% of the time
where the time goes in v3:
time: 86.7 us; the launch traced here: 86.6 us
  Pallas kernels  84.1 us (97%)
  other arithmetic  1.86 us (2%)
    pallas_call x1, Pallas kernels, per_device(): pl.pallas_call(functools.partial(kernel, total), name='tiles', out_shape=...  84.1 us
    mul x1, other arithmetic, per_device(): return (hamil * scale, corr * scale)  1.86 us

profile of v3, /device:TPU:20, one launch (start us, length us, event | category | flops | bytes accessed | tf_op | source)
XLA Modules:
  0.0 86.6 jit_solution(2148468686390801497)
XLA Ops:
  0.6 84.1 %tiles.1 = (f32[64,1024]{1,0:T(8,128)}, f32[64,1024]{1,0:T(8,128)}) custom-call(bf16[2048,256]{1,0:T(8,128)(2,1)} %r_hbm.1, bf16[2048,512]{1,0:T(8,128)(2,1)} %c_hbm.1, bf16[2048,512]{1,0:T(8,128)(2,1)} %g_hbm.1, f32[16,128]{1,0:T(8,128)} %bitcast.1), custom_call_target="tpu_custom_call" | custom-call | flops 8589934592 | bytes 6291456 | tf_op jit(solution)/shard_map/tiles/pallas_call | solution.py:410
  84.7 1.9 %broadcast_multiply_fusion = (f32[64,1024]{1,0:T(8,128)}, f32[64,1024]{1,0:T(8,128)}) fusion(f32[64,1024]{1,0:T(8,128)} %get-tuple-element.5, f32[64,1024]{1,0:T(8,128)} %get-tuple-element.4), kind=kLoop, calls=%fused_computation | loop fusion | flops 131072 | bytes 1048576 | tf_op jit(solution)/shard_map/mul | solution.py:445

commit v4 on v3

--- a/solution.py
+++ b/solution.py
@@ -33,7 +33,7 @@
     r_hbm, c_hbm, g_hbm, e_ref,
     hamil_ref, corr_ref,
     rbuf, cbuf, gbuf, cw, rt, part, csend, crecv, xsend, xown, xrecv, ysend, yrecv,
-    mown, mcore, mchip, mrecv, rmean, cmean,
+    mown, mcore, mchip, mrecv, rmean, cmean, result,
     load_sem, rsend_sem, rrecv_sem, msend_sem, mrecv_sem,
     csend_sem, crecv_sem, xsend_sem, xrecv_sem, ysend_sem, yrecv_sem,
 ):
@@ -371,6 +371,7 @@
     chip_sum(SLOT[last])
     x_sums(5)
 
+    out_copies = []
     for n, out in enumerate((corr_ref, hamil_ref)):
         for source in range(4):
             @pl.when(source != 2 * yh + p)
@@ -381,8 +382,12 @@
                     device_id=device(dp=1), device_id_type=MESH).wait_recv()
         for part_p in range(2):
             value = yrecv[part_p, n].astype(F32) + yrecv[2 + part_p, n].astype(F32)
-            out[:, part_cols[part_p]] = value
-
+            result[n, :, part_cols[part_p]] = value
+        out_copies.append(pltpu.make_async_copy(result.at[n], out, load_sem.at[n]))
+        out_copies[n].start()
+
+    for copy in out_copies:
+        copy.wait()
     for copy in started + row_copies:
         copy.wait_send()
     for n in range(2):
@@ -412,7 +417,7 @@
         name="tiles",
         out_shape=(out, out),
         in_specs=[pl.BlockSpec(memory_space=pl.ANY)] * 3 + [pl.BlockSpec(memory_space=pltpu.VMEM)],
-        out_specs=(pl.BlockSpec(memory_space=pltpu.VMEM),) * 2,
+        out_specs=(pl.BlockSpec(memory_space=pl.ANY),) * 2,
         scratch_shapes=[
             pltpu.VMEM((16, samples, 128), BF16),
             pltpu.VMEM((samples, ncols), BF16),
@@ -433,11 +438,12 @@
             pltpu.VMEM((8, 8, 128), F32),
             pltpu.VMEM((2, 4, 8, 128), F32),
             pltpu.VMEM((16, 8, 128), F32),
+            pltpu.VMEM((2, 64, width), F32),
             dma((4,)), dma((30,)), dma((16, 3)), dma((15,)), dma((15,)),
             dma((16, 2)), dma((16, 2)), dma((16, 2)), dma((4, 3, 2)), dma((4, 2)), dma((4, 2)),
         ],
         compiler_params=pltpu.CompilerParams(
-            collective_id=0, has_side_effects=True, vmem_limit_bytes=56 * 2**20),
+            collective_id=0, has_side_effects=True, vmem_limit_bytes=int(53.5 * 2**20)),
         cost_estimate=pl.CostEstimate(
             flops=2 * samples * 2048 * width, bytes_accessed=6 * 2**20, transcendentals=0),
     )(o_rows, o_cols, grad_energy, energy.reshape(samples // 128, 128))

time: 86.7 us -> 85.9 us (level)
  Pallas kernels: 84.1 us -> 82.6 us
    pallas_call x1, Pallas kernels: 84.1 us -> 82.6 us  [per_device(): pl.pallas_call(functools.partial(kernel, total), name='tiles', out_shape=...]
where the time goes in v4:
time: 85.9 us; the launch traced here: 85.7 us
  Pallas kernels  82.6 us (96%)
  other arithmetic  1.78 us (2%)
    pallas_call x1, Pallas kernels, per_device(): pl.pallas_call(functools.partial(kernel, total), name='tiles', out_shape=...  82.6 us
    mul x1, other arithmetic, per_device(): return (hamil * scale, corr * scale)  1.78 us

profile of v4, /device:TPU:20, one launch (start us, length us, event | category | flops | bytes accessed | tf_op | source)
XLA Modules:
  0.0 85.7 jit_solution(5470869490656061205)
XLA Ops:
  0.6 0.0 copy-start
  0.6 0.7 copy-done
  1.3 82.6 %tiles.1 = (f32[64,1024]{1,0:T(8,128)S(1)}, f32[64,1024]{1,0:T(8,128)}) custom-call(bf16[2048,256]{1,0:T(8,128)(2,1)} %r_hbm.1, bf16[2048,512]{1,0:T(8,128)(2,1)} %c_hbm.1, bf16[2048,512]{1,0:T(8,128)(2,1)} %g_hbm.1, f32[16,128]{1,0:T(8,128)S(1)} %bitcast.1), custom_call_target="tpu_custom_call" | custom-call | flops 8589934592 | bytes 6291456 | tf_op jit(solution)/shard_map/tiles/pallas_call | solution.py:415
  83.9 1.8 %broadcast_multiply_fusion = (f32[64,1024]{1,0:T(8,128)}, f32[64,1024]{1,0:T(8,128)}) fusion(f32[64,1024]{1,0:T(8,128)} %get-tuple-element.5, f32[64,1024]{1,0:T(8,128)S(1)} %get-tuple-element.4), kind=kLoop, calls=%fused_computation | loop fusion | flops 131072 | bytes 1048576 | tf_op jit(solution)/shard_map/mul | solution.py:451
Async XLA Ops:
  0.6 0.7 copy-start
